TPU v7x, 128 devices: a whole 4x4x4 slice. The times are simulated.
128 devices in a mesh: ctx: 8 (over x_hi, y), head: 8 (over z, core), var: 2 (over x_lo).
Axes of the slice: x: 4 (x_hi: 2, x_lo: 2; x = x_hi * 2 + x_lo), y: 4, z: 4, core: 2. Of those that a mesh axis runs over, the one named last changes fastest.
Arguments:
- sequence: bfloat16 [4096, 1536], P('ctx', 'head'), may hold values from -8 to 8
- deletions: int32 [8, 2], P('var'), parts along dimension 0, may hold values from 0 to 4096, as said below
- conv_taps: float32 [3, 1536], P(None, 'head'), may hold values from -3 to 3
- conv_bias: float32 [1536], P('head'), may hold values from -3 to 3
- w_proj: bfloat16 [1536, 3584], P(None, 'head'), may hold values from -1 to 1
- w_out: bfloat16 [1536, 1536], P('head'), may hold values from -0.15625 to 0.15625
- w_pair: bfloat16 [1536, 256], P('head'), may hold values from -0.15625 to 0.15625
- dist_table: float32 [16, 128], replicated, may hold values from -3 to 3
Outputs:
- pair_map: bfloat16 [8, 1024, 1024, 128], P('var', 'ctx', 'head'), parts along dimension 0
There are 2 independent parts, one for each index of `var`. A program takes and returns all parts, laid end to end along the dimension named above; an argument that names none is the same for every part. Nothing has to cross between parts.
Inputs may be any that keep to these rules, and one draw needn't show every extreme that they name: `deletions`: each variant deletes 1 to 128 consecutive tokens, some variant deletes exactly 128, and some variant's deletion ends at the last token of the locus.
All inputs are finite; a program needn't handle non-finite values.
Results may differ from a plain program's by a relative error of at most 0.025.
Values may be sent and summed in bfloat16 or wider, within the bound.
A program may use at most 128 MiB of HBM per device.

v0:
```python
import math
import jax
import jax.numpy as jnp
from jax import lax
from jax.sharding import PartitionSpec as P

HD = 128
VD = 192
C = 128
NB = 16
POOL = 4


def extended(block, sides, width):
    for axis, dim in sides:
        count = lax.axis_size(axis)
        forward = [(i, i + 1) for i in range(count - 1)]
        backward = [(target, source) for source, target in forward]
        low = lax.ppermute(
            lax.slice_in_dim(block, block.shape[dim] - width, None, axis=dim), axis, forward
        )
        high = lax.ppermute(lax.slice_in_dim(block, 0, width, axis=dim), axis, backward)
        block = jnp.concatenate([low, block, high], axis=dim)
    return block


def attend_block(running, queries, key_rows, value_rows):
    row_max, row_sum, weighted = running
    scores = jnp.einsum(
        "vqhe,vkhe->vhqk", queries, key_rows, preferred_element_type=jnp.float32
    ) / math.sqrt(queries.shape[-1])
    new_max = jnp.maximum(row_max, scores.max(-1))
    shrink = jnp.exp(row_max - new_max)
    weights = jnp.exp(scores - new_max[..., None])
    row_sum = row_sum * shrink + weights.sum(-1)
    weighted = weighted * shrink[..., None] + jnp.einsum(
        "vhqk,vkhe->vhqe",
        weights.astype(jnp.bfloat16),
        value_rows,
        preferred_element_type=jnp.float32,
    )
    return (new_max, row_sum, weighted)


def attend_rows(running, queries, key_rows, value_rows):
    key_total = key_rows.shape[1]
    block_rows = 512
    block_count = key_total // block_rows

    def block_step(block_index, state_now):
        key_part = lax.dynamic_slice_in_dim(key_rows, block_index * block_rows, block_rows, 1)
        value_part = lax.dynamic_slice_in_dim(value_rows, block_index * block_rows, block_rows, 1)
        return attend_block(state_now, queries, key_part, value_part)

    return lax.fori_loop(0, block_count, block_step, running)


def local(sequence, deletions, conv_taps, conv_bias, w_proj, w_out, w_pair, dist_table):
    token_count, local_width = sequence.shape
    variants = deletions.shape[0]
    head_count = w_out.shape[0] // VD
    row_start = lax.axis_index("ctx") * token_count
    positions = row_start + jnp.arange(token_count, dtype=jnp.int32)
    kept = jnp.logical_or(
        positions[None, :] < deletions[:, 0:1], positions[None, :] >= deletions[:, 1:2]
    )
    masked = jnp.where(kept[:, :, None], sequence[None], jnp.zeros((), jnp.bfloat16))
    dilation = token_count // 2
    padded = extended(masked, (("ctx", 1),), dilation)
    spread = padded.astype(jnp.float32)
    middle = spread[:, dilation : dilation + token_count]
    convolved = (
        conv_taps[0] * spread[:, :token_count]
        + conv_taps[1] * middle
        + conv_taps[2] * spread[:, 2 * dilation : 2 * dilation + token_count]
        + conv_bias
    )
    trunk_out = (middle + jax.nn.gelu(convolved, approximate=True)).astype(jnp.bfloat16)
    projected = jnp.einsum(
        "vtd,df->vtf",
        lax.all_gather(trunk_out, "head", axis=2, tiled=True),
        w_proj,
        preferred_element_type=jnp.float32,
    ).astype(jnp.bfloat16)
    projected = projected.reshape(trunk_out.shape[0], token_count, head_count, 2 * HD + VD)
    queries = projected[:variants, :, :, :HD]
    key_rows = projected[:, :, :, HD : 2 * HD]
    value_rows = projected[:, :, :, 2 * HD :]
    running = attend_rows(
        (
            jnp.full((variants, head_count, token_count), -jnp.inf, jnp.float32),
            jnp.zeros((variants, head_count, token_count), jnp.float32),
            jnp.zeros((variants, head_count, token_count, VD), jnp.float32),
        ),
        queries,
        lax.all_gather(key_rows, "ctx", axis=1, tiled=True),
        lax.all_gather(value_rows, "ctx", axis=1, tiled=True),
    )
    row_max, row_sum, weighted = running
    head_out = (weighted / row_sum[..., None]).astype(jnp.bfloat16)
    flat_out = head_out.transpose(0, 2, 1, 3).reshape(variants * token_count, head_count * VD)
    mixed_back = lax.psum_scatter(
        lax.dot_general(
            w_out, flat_out, (((0,), (1,)), ((), ())), preferred_element_type=jnp.float32
        ).astype(jnp.bfloat16),
        "head",
        scatter_dimension=0,
        tiled=True,
    ).astype(jnp.float32)
    residual = trunk_out.astype(jnp.float32) + mixed_back.T.reshape(
        variants, token_count, local_width
    )
    pooled = (
        residual.reshape(variants, token_count // POOL, POOL, local_width)
        .mean(2)
        .astype(jnp.bfloat16)
    )
    partial_value = jnp.einsum("vpd,dc->vpc", pooled, w_pair, preferred_element_type=jnp.float32)
    pair_proj = lax.psum(partial_value.astype(jnp.bfloat16), "head").astype(jnp.float32)
    row_feats = pair_proj[:, :, :C]
    all_cols = lax.all_gather(
        pair_proj[:, :, C:].astype(jnp.bfloat16), "ctx", axis=1, tiled=True
    ).astype(jnp.float32)
    col_count = all_cols.shape[1] // lax.axis_size("head")
    col_start = lax.axis_index("head") * col_count
    col_feats = lax.dynamic_slice_in_dim(all_cols, col_start, col_count, 1)
    row_ids = lax.axis_index("ctx") * (token_count // POOL) + jnp.arange(
        token_count // POOL, dtype=jnp.int32
    )
    col_ids = col_start + jnp.arange(col_count, dtype=jnp.int32)
    distance = jnp.abs(row_ids[:, None] - col_ids[None, :])
    buckets = jnp.zeros(distance.shape, jnp.int32)
    for power_index in range(NB - 1):
        buckets = buckets + (distance >= 2**power_index).astype(jnp.int32)
    one_hot = (buckets[:, :, None] == jnp.arange(NB, dtype=jnp.int32)).astype(jnp.float32)
    rel_table = jnp.dot(one_hot, dist_table, precision=lax.Precision.HIGHEST)
    pair_map = row_feats[:, :, None, :] + col_feats[:, None, :, :] + rel_table[None]
    return pair_map.astype(jnp.bfloat16)


def solution(mesh):
    in_specs = (
        P("ctx", "head"),
        P("var", None),
        P(None, "head"),
        P("head"),
        P(None, "head"),
        P("head", None),
        P("head", None),
        P(),
    )
    out_specs = P("var", "ctx", "head", None)
    return jax.shard_map(local, mesh=mesh, in_specs=in_specs, out_specs=out_specs, check_vma=False)
```

profile of v0, /device:TPU:0, one launch (start us, length us, event | category | flops | bytes accessed | tf_op | source)
XLA Modules:
  0.0 486.1 jit_solution(6132765217847577570)
XLA Ops:
  8.5 3.6 collective-permute-start
  13.4 7.0 %collective-permute-done = bf16[4,256,192]{1,2,0:T(8,128)(2,1)S(1)} collective-permute-done((bf16[4,256,192]{1,2,0:T(8,128)(2,1)S(1)}, bf16[4,256,192]{1,2,0:T(8,128)(2,1)S(1)}, u32[]{:S(2)}, u32[]{:S(2)}) %collective-permute-start) | collective-permute-done | bytes 393248 | tf_op jit(solution)/shard_map/ppermute | solution.py:19
  20.4 4.1 collective-permute-done.1
  28.8 45.7 %all-gather.5.cloned.1.call-done = bf16[4,512,1536]{1,2,0:T(8,128)(2,1)} async-done(((bf16[4,512,192]{1,2,0:T(8,128)(2,1)}), bf16[4,512,1536]{1,2,0:T(8,128)(2,1)}) %all-gather.5.cloned.1.call-update) | async-done | bytes 6291472 | tf_op jit(solution)/shard_map/all_gather | solution.py:81
  74.5 5.8 %convert_bitcast_fusion = bf16[4,512,1,448]{1,3,0,2:T(8,128)(2,1)S(1)} fusion(bf16[4,512,1536]{1,2,0:T(8,128)(2,1)} %all-gather.5.cloned.1.call-done, bf16[1536,448]{0,1:T(8,128)(2,1)S(1)} %copy-done), kind=kOutput, calls=%fused_computation.29 | convolution fusion | flops 2819489792 | bytes 9502720 | tf_op jit(solution)/shard_map/vtd,df->vtf/dot_general | solution.py:79
  85.0 71.1 %all-gather.7.cloned.1.call-done = bf16[4,4096,1,128]{1,3,0,2:T(8,128)(2,1)} async-done(((bf16[4,512,1,128]{1,3,0,2:T(8,128)(2,1)}), bf16[4,4096,1,128]{1,3,0,2:T(8,128)(2,1)}) %all-gather.7.cloned.1.call-update) | async-done | bytes 4194320 | tf_op jit(solution)/shard_map/all_gather | solution.py:96
  156.1 93.5 %all-gather.9.cloned.1.call-done = bf16[4,4096,1,192]{1,3,0,2:T(8,128)(2,1)} async-done(((bf16[4,512,1,192]{1,3,0,2:T(8,128)(2,1)}), bf16[4,4096,1,192]{1,3,0,2:T(8,128)(2,1)}) %all-gather.9.cloned.1.call-update) | async-done | bytes 6291472 | tf_op jit(solution)/shard_map/all_gather | solution.py:97
  249.6 40.1 %while.18 = (s32[]{:T(128)}, f32[4,1,512]{2,0,1:T(4,128)S(1)}, f32[4,1,512]{2,0,1:T(4,128)S(1)}, f32[4,1,512,192]{2,3,0,1:T(8,128)S(1)}, bf16[4,4096,1,128]{1,3,...) while((s32[]{:T(128)}, f32[4,1,512]{2,0,1:T(4,128)S(1)}, ...), condition=%wide.region_3.4_spmd.clone, body=%wide.region_0.3_spmd.clone.sunk | while | flops 680669184 | bytes 17694904 | solution.py:55
  252.1 2.4 bitcast_add_fusion.5
  257.1 2.4 bitcast_add_fusion.5
  262.2 2.4 bitcast_add_fusion.5
  267.2 2.4 bitcast_add_fusion.5
  272.2 2.4 bitcast_add_fusion.5
  277.2 2.4 bitcast_add_fusion.5
  287.3 2.4 bitcast_add_fusion.5
  291.0 4.5 fusion.19
  295.6 8.7 %copy.38 = bf16[1536,2048]{1,0:T(8,128)(2,1)} copy(bf16[1536,2048]{0,1:T(8,128)(2,1)} %fusion.19) | data formatting | bytes 12582912
  304.5 40.6 %reduce-scatter.4.cloned.1.call-done = bf16[192,2048]{1,0:T(8,128)(2,1)} async-done(((bf16[1536,2048]{1,0:T(8,128)(2,1)}), bf16[192,2048]{1,0:T(8,128)(2,1)}) %reduce-scatter.4.cloned.1.call-update) | async-done | bytes 786448
  348.0 2.9 copy.32
  351.0 3.6 convert_add_fusion
  358.5 59.7 %all-reduce.2.cloned.1.call-done = bf16[4,128,256]{2,1,0:T(8,128)(2,1)} async-done(((bf16[4,128,256]{2,1,0:T(8,128)(2,1)}), bf16[4,128,256]{2,1,0:T(8,128)(2,1)}) %all-reduce.2.cloned.1.call-update) | async-done | bytes 262160 | tf_op jit(solution)/shard_map/psum | solution.py:119
  420.1 8.9 %fusion.33 = f32[128,128,128]{2,1,0:T(8,128)} fusion(s32[128,128]{1,0:T(8,128)S(1)} %convert_add_fusion.1, f32[16,128]{1,0:T(8,128)S(1)} %copy-done.7), kind=kOutput, calls=%fused_computation.50 | convolution fusion | flops 402915328 | bytes 8462336 | tf_op jit(solution)/shard_map/dot_general | solution.py:136
  429.0 36.8 %all-gather.11.cloned.1.call-done = bf16[4,1024,128]{2,1,0:T(8,128)(2,1)} async-done(((bf16[4,128,128]{2,1,0:T(8,128)(2,1)}), bf16[4,1024,128]{2,1,0:T(8,128)(2,1)}) %all-gather.11.cloned.1.call-update) | async-done | bytes 1048592 | tf_op jit(solution)/shard_map/all_gather | solution.py:121
  466.8 12.4 %add_convert_fusion = bf16[4,128,128,128]{3,2,1,0:T(8,128)(2,1)} fusion(f32[128,128,128]{2,1,0:T(8,128)} %fusion.33, f32[4,128,128]{2,1,0:T(8,128)S(1)} %dynamic-slice_convert_fusion, f32[4,128,128]{2,1,0:T(8,128)S(1)} %get-tuple-element.206), kind=kLoop, calls=%fused_computation.24 | loop fusion | flops 25165824 | bytes 25690112 | tf_op jit(solution)/shard_map/convert_element_type | solution.py:138
  (101 shorter events, 46.0 us)
Async XLA Ops:
  6.5 68.0 %copy-start = (bf16[1536,448]{0,1:T(8,128)(2,1)S(1)}, bf16[1536,448]{0,1:T(8,128)(2,1)}, u32[]{:S(2)}) copy-start(bf16[1536,448]{0,1:T(8,128)(2,1)} %param.14) | copy-start | bytes 4128772
  6.5 6.9 %copy-start.9 = (f32[3,192]{1,0:T(4,128)S(1)}, f32[3,192]{1,0:T(4,128)}, u32[]{:S(2)}) copy-start(f32[3,192]{1,0:T(4,128)} %param.12) | copy-start | bytes 6916
  6.5 68.0 %all-gather.5.cloned.1.call-start = ((), (), s32[]{:S(2)}) async-start(), calls=%async_computation.1 | async-start | bytes 7077888 | tf_op jit(solution)/shard_map/all_gather | solution.py:81
  8.5 11.9 %collective-permute-start = (bf16[4,256,192]{1,2,0:T(8,128)(2,1)S(1)}, bf16[4,256,192]{1,2,0:T(8,128)(2,1)S(1)}, u32[]{:S(2)}, u32[]{:S(2)}) collective-permute-start(bf16[4,256,192]{1,2,0:T(8,128)(2,1)S(1)} %get-tuple-element.204), channel_id=1, source_target_pairs={{0,16},{16,32},{32,48},{48,64},{64,80},{80,96},{96,112},{1,17},{17... | collective-permute-start | bytes 1179656 | tf_op jit(solution)/shard_map/ppermute | solution.py:19
  12.1 12.5 %collective-permute-start.1 = (bf16[4,256,192]{1,2,0:T(8,128)(2,1)S(1)}, bf16[4,256,192]{1,2,0:T(8,128)(2,1)S(1)}, u32[]{:S(2)}, u32[]{:S(2)}) collective-permute-start(bf16[4,256,192]{1,2,0:T(8,128)(2,1)S(1)} %get-tuple-element.205), channel_id=1, source_target_pairs={{16,0},{32,16},{48,32},{64,48},{80,64},{96,80},{112,96},{17,1},{33... | collective-permute-start | bytes 1179656 | tf_op jit(solution)/shard_map/ppermute | solution.py:22
  13.4 13.4 %copy-start.8 = (f32[192]{0:T(256)S(1)}, f32[192]{0:T(256)}, u32[]{:S(2)}) copy-start(f32[192]{0:T(256)} %param.13) | copy-start | bytes 2308
  25.0 1.8 copy-start.2
  28.8 127.3 %all-gather.7.cloned.1.call-start = ((), (), s32[]{:S(2)}) async-start(), calls=%async_computation.2 | async-start | bytes 4718592 | tf_op jit(solution)/shard_map/all_gather | solution.py:96
  80.3 1.2 copy-start.4
  82.4 167.1 %all-gather.9.cloned.1.call-start = ((), (), s32[]{:S(2)}) async-start(), calls=%async_computation.3 | async-start | bytes 7077888 | tf_op jit(solution)/shard_map/all_gather | solution.py:97
  84.6 260.5 %reduce-scatter.4.cloned.1.call-start = ((), (), s32[]{:S(2)}) async-start(), calls=%async_computation.6 | async-start | bytes 7077888
  289.9 1.1 copy-start.5
  304.3 113.9 %all-reduce.2.cloned.1.call-start = ((), (), s32[]{:S(2)}) async-start(), calls=%async_computation.4 | async-start | bytes 524288 | tf_op jit(solution)/shard_map/psum | solution.py:119
  348.0 2.9 copy-start.3
  356.6 0.9 copy-start.6
  357.2 63.0 %copy-start.7 = (f32[16,128]{1,0:T(8,128)S(1)}, f32[16,128]{1,0:T(8,128)}, u32[]{:S(2)}) copy-start(f32[16,128]{1,0:T(8,128)} %param.17) | copy-start | bytes 24580
  358.5 107.4 %all-gather.11.cloned.1.call-start = ((), (), s32[]{:S(2)}) async-start(), calls=%async_computation.5 | async-start | bytes 1179648 | tf_op jit(solution)/shard_map/all_gather | solution.py:121
  466.8 12.4 %copy-start.1 = (bf16[1536,448]{0,1:T(8,128)(2,1)S(1)}, bf16[1536,448]{0,1:T(8,128)(2,1)}, u32[]{:S(2)}) copy-start(bf16[1536,448]{0,1:T(8,128)(2,1)} %param.14) | copy-start | bytes 4128772
Sparse Core Ops, SparseCore 0:
  28.9 45.5 all-gather.4
  82.6 73.4 all-gather.6
  158.3 91.2 all-gather.8
  304.4 40.6 reduce-scatter.3
  358.6 59.6 all-reduce.1
  420.7 45.1 all-gather.10
where the time goes:
time: 488 us; the launch traced here: 486 us
  waiting for transfers between devices  359 us (74%)
  matrix products  54 us (11%)
  other arithmetic  30.4 us (6%)
  local copies, waits for them, and re-layouts  23.6 us (5%)
  between operations  13.7 us (3%)
  starting transfers between devices  5.27 us (1%)
    all_gather x1, waiting for transfers between devices, local(): lax.all_gather(value_rows, 'ctx', axis=1, tiled=True)  93.5 us
    all_gather x1, waiting for transfers between devices, local(): lax.all_gather(key_rows, 'ctx', axis=1, tiled=True)  71.1 us
    psum x1, waiting for transfers between devices, local(): lax.psum(partial_value.astype(jnp.bfloat16), 'head').astype(jnp.float32)  59.7 us
    all_gather x1, waiting for transfers between devices, local(): lax.all_gather(trunk_out, 'head', axis=2, tiled=True)  45.7 us
    unnamed x7, waiting for transfers between devices  40.6 us
    all_gather x1, waiting for transfers between devices, local(): lax.all_gather(pair_proj[:, :, C:].astype(jnp.bfloat16), 'ctx', axis=1, t...  36.8 us
    dot_general x8, matrix products, attend_block(): jnp.einsum('vhqk,vkhe->vhqe', weights.astype(jnp.bfloat16), value_rows, p...  19.3 us
    dot_general x8, matrix products, attend_block(): jnp.einsum('vqhe,vkhe->vhqk', queries, key_rows, preferred_element_type=j...  14.5 us
  transfers between devices with their start and end apart: 8, of which 8 were waited for; matrix products, arithmetic and copies ran while one was open for 2% of the time, Pallas kernels for 0%

commit v1 on v0

--- a/solution.py
+++ b/solution.py
@@ -116,7 +116,8 @@
         .astype(jnp.bfloat16)
     )
     partial_value = jnp.einsum("vpd,dc->vpc", pooled, w_pair, preferred_element_type=jnp.float32)
-    pair_proj = lax.psum(partial_value.astype(jnp.bfloat16), "head").astype(jnp.float32)
+    start_loads = lambda vals: jnp.sum(jax.lax.all_gather(vals, "head"), axis=0)
+    pair_proj = start_loads(partial_value.astype(jnp.bfloat16)).astype(jnp.float32)
     row_feats = pair_proj[:, :, :C]
     all_cols = lax.all_gather(
         pair_proj[:, :, C:].astype(jnp.bfloat16), "ctx", axis=1, tiled=True

time: 488 us -> 455 us (0.932)
  waiting for transfers between devices: 359 us -> 325 us
    psum x1 -> x0, waiting for transfers between devices: 59.7 us -> none  [local(): lax.psum(partial_value.astype(jnp.bfloat16), 'head').astype(jnp.float32)]
    all_gather x0 -> x1, waiting for transfers between devices: none -> 25.1 us  [local(): start_loads = lambda vals: jnp.sum(jax.lax.all_gather(vals, 'head'), axis=0)]
  transfers between devices with their start and end apart: 8 -> 8, of which waited for: 8 -> 8; matrix products, arithmetic and copies ran while one was open for 2% -> 3% of each run, Pallas kernels for 0% -> 0%
where the time goes in v1:
time: 455 us; the launch traced here: 453 us
  waiting for transfers between devices  325 us (71%)
  matrix products  54 us (12%)
  other arithmetic  31.4 us (7%)
  local copies, waits for them, and re-layouts  23.6 us (5%)
  between operations  13.7 us (3%)
  starting transfers between devices  5.27 us (1%)
    all_gather x1, waiting for transfers between devices, local(): lax.all_gather(value_rows, 'ctx', axis=1, tiled=True)  93.5 us
    all_gather x1, waiting for transfers between devices, local(): lax.all_gather(key_rows, 'ctx', axis=1, tiled=True)  71.1 us
    all_gather x1, waiting for transfers between devices, local(): lax.all_gather(trunk_out, 'head', axis=2, tiled=True)  45.7 us
    unnamed x7, waiting for transfers between devices  40.6 us
    all_gather x1, waiting for transfers between devices, local(): lax.all_gather(pair_proj[:, :, C:].astype(jnp.bfloat16), 'ctx', axis=1, t...  37.6 us
    all_gather x1, waiting for transfers between devices, local(): start_loads = lambda vals: jnp.sum(jax.lax.all_gather(vals, 'head'), axis=0)  25.1 us
    dot_general x8, matrix products, attend_block(): jnp.einsum('vhqk,vkhe->vhqe', weights.astype(jnp.bfloat16), value_rows, p...  19.3 us
    dot_general x8, matrix products, attend_block(): jnp.einsum('vqhe,vkhe->vhqk', queries, key_rows, preferred_element_type=j...  14.5 us
  transfers between devices with their start and end apart: 8, of which 8 were waited for; matrix products, arithmetic and copies ran while one was open for 3% of the time, Pallas kernels for 0%

profile of v1, /device:TPU:0, one launch (start us, length us, event | category | flops | bytes accessed | tf_op | source)
XLA Modules:
  0.0 453.2 jit_solution(3893172955179409513)
XLA Ops:
  8.5 3.6 collective-permute-start
  13.4 7.0 %collective-permute-done = bf16[4,256,192]{1,2,0:T(8,128)(2,1)S(1)} collective-permute-done((bf16[4,256,192]{1,2,0:T(8,128)(2,1)S(1)}, bf16[4,256,192]{1,2,0:T(8,128)(2,1)S(1)}, u32[]{:S(2)}, u32[]{:S(2)}) %collective-permute-start) | collective-permute-done | bytes 393248 | tf_op jit(solution)/shard_map/ppermute | solution.py:19
  20.4 4.1 collective-permute-done.1
  28.8 45.7 %all-gather.7.cloned.1.call-done = bf16[4,512,1536]{1,2,0:T(8,128)(2,1)} async-done(((bf16[4,512,192]{1,2,0:T(8,128)(2,1)}), bf16[4,512,1536]{1,2,0:T(8,128)(2,1)}) %all-gather.7.cloned.1.call-update) | async-done | bytes 6291472 | tf_op jit(solution)/shard_map/all_gather | solution.py:81
  74.5 5.8 %convert_bitcast_fusion = bf16[4,512,1,448]{1,3,0,2:T(8,128)(2,1)S(1)} fusion(bf16[4,512,1536]{1,2,0:T(8,128)(2,1)} %all-gather.7.cloned.1.call-done, bf16[1536,448]{0,1:T(8,128)(2,1)S(1)} %copy-done), kind=kOutput, calls=%fused_computation.29 | convolution fusion | flops 2819489792 | bytes 9502720 | tf_op jit(solution)/shard_map/vtd,df->vtf/dot_general | solution.py:79
  85.0 71.1 %all-gather.9.cloned.1.call-done = bf16[4,4096,1,128]{1,3,0,2:T(8,128)(2,1)} async-done(((bf16[4,512,1,128]{1,3,0,2:T(8,128)(2,1)}), bf16[4,4096,1,128]{1,3,0,2:T(8,128)(2,1)}) %all-gather.9.cloned.1.call-update) | async-done | bytes 4194320 | tf_op jit(solution)/shard_map/all_gather | solution.py:96
  156.1 93.5 %all-gather.11.cloned.1.call-done = bf16[4,4096,1,192]{1,3,0,2:T(8,128)(2,1)} async-done(((bf16[4,512,1,192]{1,3,0,2:T(8,128)(2,1)}), bf16[4,4096,1,192]{1,3,0,2:T(8,128)(2,1)}) %all-gather.11.cloned.1.call-update) | async-done | bytes 6291472 | tf_op jit(solution)/shard_map/all_gather | solution.py:97
  249.6 40.1 %while.18 = (s32[]{:T(128)}, f32[4,1,512]{2,0,1:T(4,128)S(1)}, f32[4,1,512]{2,0,1:T(4,128)S(1)}, f32[4,1,512,192]{2,3,0,1:T(8,128)S(1)}, bf16[4,4096,1,128]{1,3,...) while((s32[]{:T(128)}, f32[4,1,512]{2,0,1:T(4,128)S(1)}, ...), condition=%wide.region_3.4_spmd.clone, body=%wide.region_0.3_spmd.clone.sunk | while | flops 680669184 | bytes 17694904 | solution.py:55
  252.1 2.4 bitcast_add_fusion.5
  257.1 2.4 bitcast_add_fusion.5
  262.2 2.4 bitcast_add_fusion.5
  267.2 2.4 bitcast_add_fusion.5
  272.2 2.4 bitcast_add_fusion.5
  277.2 2.4 bitcast_add_fusion.5
  287.3 2.4 bitcast_add_fusion.5
  291.0 4.5 %fusion.19 = bf16[1536,2048]{0,1:T(8,128)(2,1)} fusion(bf16[2048,192]{0,1:T(8,128)(2,1)S(1)} %bitcast.95, bf16[192,1536]{1,0:T(8,128)(2,1)S(1)} %copy-done.5), kind=kOutput, calls=%fused_computation.26 | convolution fusion | flops 1211105280 | bytes 7667712 | tf_op jit(solution)/shard_map/dot_general | solution.py:103
  295.6 8.7 %copy.38 = bf16[1536,2048]{1,0:T(8,128)(2,1)} copy(bf16[1536,2048]{0,1:T(8,128)(2,1)} %fusion.19) | data formatting | bytes 12582912
  304.5 40.6 %reduce-scatter.4.cloned.1.call-done = bf16[192,2048]{1,0:T(8,128)(2,1)} async-done(((bf16[1536,2048]{1,0:T(8,128)(2,1)}), bf16[192,2048]{1,0:T(8,128)(2,1)}) %reduce-scatter.4.cloned.1.call-update) | async-done | bytes 786448
  348.0 2.9 copy.32
  351.0 3.6 convert_add_fusion
  358.5 25.1 %all-gather.15.cloned.1.call-done = bf16[32,128,256]{2,1,0:T(8,128)(2,1)} async-done(((bf16[4,128,256]{2,1,0:T(8,128)(2,1)}), bf16[32,128,256]{2,1,0:T(8,128)(2,1)}) %all-gather.15.cloned.1.call-update) | async-done | bytes 2097168 | tf_op jit(solution)/shard_map/all_gather | solution.py:119
  386.4 8.9 %fusion.33 = f32[128,128,128]{2,1,0:T(8,128)} fusion(s32[128,128]{1,0:T(8,128)S(1)} %convert_add_fusion.1, f32[16,128]{1,0:T(8,128)S(1)} %copy-done.7), kind=kOutput, calls=%fused_computation.50 | convolution fusion | flops 402915328 | bytes 8462336 | tf_op jit(solution)/shard_map/dot_general | solution.py:137
  395.3 37.6 %all-gather.13.cloned.1.call-done = bf16[4,1024,128]{2,1,0:T(8,128)(2,1)} async-done(((bf16[4,128,128]{2,1,0:T(8,128)(2,1)}), bf16[4,1024,128]{2,1,0:T(8,128)(2,1)}) %all-gather.13.cloned.1.call-update) | async-done | bytes 1048592 | tf_op jit(solution)/shard_map/all_gather | solution.py:122
  433.9 12.4 %add_convert_fusion = bf16[4,128,128,128]{3,2,1,0:T(8,128)(2,1)} fusion(f32[128,128,128]{2,1,0:T(8,128)} %fusion.33, f32[4,128,128]{2,1,0:T(8,128)S(1)} %dynamic-slice_convert_fusion, f32[4,128,128]{2,1,0:T(8,128)S(1)} %get-tuple-element.206), kind=kLoop, calls=%fused_computation.24 | loop fusion | flops 25165824 | bytes 25690112 | tf_op jit(solution)/shard_map/convert_element_type | solution.py:139
  (102 shorter events, 47.0 us)
Async XLA Ops:
  6.5 68.0 %copy-start = (bf16[1536,448]{0,1:T(8,128)(2,1)S(1)}, bf16[1536,448]{0,1:T(8,128)(2,1)}, u32[]{:S(2)}) copy-start(bf16[1536,448]{0,1:T(8,128)(2,1)} %param.14) | copy-start | bytes 4128772
  6.5 6.9 %copy-start.9 = (f32[3,192]{1,0:T(4,128)S(1)}, f32[3,192]{1,0:T(4,128)}, u32[]{:S(2)}) copy-start(f32[3,192]{1,0:T(4,128)} %param.12) | copy-start | bytes 6916
  6.5 68.0 %all-gather.7.cloned.1.call-start = ((), (), s32[]{:S(2)}) async-start(), calls=%async_computation.1 | async-start | bytes 7077888 | tf_op jit(solution)/shard_map/all_gather | solution.py:81
  8.5 11.9 %collective-permute-start = (bf16[4,256,192]{1,2,0:T(8,128)(2,1)S(1)}, bf16[4,256,192]{1,2,0:T(8,128)(2,1)S(1)}, u32[]{:S(2)}, u32[]{:S(2)}) collective-permute-start(bf16[4,256,192]{1,2,0:T(8,128)(2,1)S(1)} %get-tuple-element.204), channel_id=1, source_target_pairs={{0,16},{16,32},{32,48},{48,64},{64,80},{80,96},{96,112},{1,17},{17... | collective-permute-start | bytes 1179656 | tf_op jit(solution)/shard_map/ppermute | solution.py:19
  12.1 12.5 %collective-permute-start.1 = (bf16[4,256,192]{1,2,0:T(8,128)(2,1)S(1)}, bf16[4,256,192]{1,2,0:T(8,128)(2,1)S(1)}, u32[]{:S(2)}, u32[]{:S(2)}) collective-permute-start(bf16[4,256,192]{1,2,0:T(8,128)(2,1)S(1)} %get-tuple-element.205), channel_id=1, source_target_pairs={{16,0},{32,16},{48,32},{64,48},{80,64},{96,80},{112,96},{17,1},{33... | collective-permute-start | bytes 1179656 | tf_op jit(solution)/shard_map/ppermute | solution.py:22
  13.4 13.4 %copy-start.8 = (f32[192]{0:T(256)S(1)}, f32[192]{0:T(256)}, u32[]{:S(2)}) copy-start(f32[192]{0:T(256)} %param.13) | copy-start | bytes 2308
  25.0 1.8 copy-start.2
  28.8 127.3 %all-gather.9.cloned.1.call-start = ((), (), s32[]{:S(2)}) async-start(), calls=%async_computation.2 | async-start | bytes 4718592 | tf_op jit(solution)/shard_map/all_gather | solution.py:96
  80.3 1.2 copy-start.4
  82.4 167.1 %all-gather.11.cloned.1.call-start = ((), (), s32[]{:S(2)}) async-start(), calls=%async_computation.3 | async-start | bytes 7077888 | tf_op jit(solution)/shard_map/all_gather | solution.py:97
  84.6 260.5 %reduce-scatter.4.cloned.1.call-start = ((), (), s32[]{:S(2)}) async-start(), calls=%async_computation.6 | async-start | bytes 7077888
  289.9 1.1 copy-start.5
  304.3 79.2 %all-gather.15.cloned.1.call-start = ((), (), s32[]{:S(2)}) async-start(), calls=%async_computation.5 | async-start | bytes 2359296 | tf_op jit(solution)/shard_map/all_gather | solution.py:119
  348.0 2.9 copy-start.3
  356.6 0.9 copy-start.6
  358.5 74.5 %all-gather.13.cloned.1.call-start = ((), (), s32[]{:S(2)}) async-start(), calls=%async_computation.4 | async-start | bytes 1179648 | tf_op jit(solution)/shard_map/all_gather | solution.py:122
  383.6 2.9 copy-start.7
  433.9 12.4 %copy-start.1 = (bf16[1536,448]{0,1:T(8,128)(2,1)S(1)}, bf16[1536,448]{0,1:T(8,128)(2,1)}, u32[]{:S(2)}) copy-start(bf16[1536,448]{0,1:T(8,128)(2,1)} %param.14) | copy-start | bytes 4128772
Sparse Core Ops, SparseCore 0:
  28.9 45.5 all-gather.6
  82.6 73.4 all-gather.8
  158.3 91.2 all-gather.10
  304.4 40.6 reduce-scatter.3
  358.6 24.9 all-gather.14
  386.3 46.5 all-gather.12
